TPU v7x, 32 devices: a whole 2x2x4 slice. The times are simulated.
32 devices in a mesh: comp: 8 (over z, y), tile: 4 (over x, core).
Axes of the slice: x: 2, y: 2, z: 4, core: 2. Of those that a mesh axis runs over, the one named last changes fastest.
Arguments:
- spectrum: float32 [1152, 8192], P('comp', 'tile'), may hold values from 0.015 to 18, as said below
- depth: float32 [8192], P('tile'), may hold values from 5 to 4000
- currents: float32 [2, 8192], P(None, 'tile'), may hold values from -3 to 3
- winds: float32 [2, 8192], P(None, 'tile'), may hold values from -24 to 24
- sea_mask: int32 [8192], P('tile'), may hold values from 0 to 1
- neighbours: int32 [4, 8192], P(None, 'tile'), may hold values from 0 to 2304, as said below
- interaction: bfloat16 [1152, 1152], replicated, may hold values from -0.1875 to 0.1875
Outputs:
- spectrum_next: float32 [1152, 8192], P('comp', 'tile')
Inputs may be any that keep to these rules, and one draw needn't show every extreme that they name: `spectrum`: positive everywhere. `neighbours`: for a cell at position q within its tile, entry j is either the fixed position 128 + q + 1, 128 + q - 1, 256 + q or q (for j = 0, 1, 2, 3), when that neighbour is a sea cell inside the grid, or else 2048 + 2 * 128.
All inputs are finite; a program needn't handle non-finite values.
Results may differ from a plain program's by a relative error of at most 0.00039.
The roundings to bfloat16 on the way count: a program that leaves them out, or rounds other values in their place, can miss the bound.
Values sent between devices are 32-bit elements; how exact they have to be, the bound alone decides.
A program may use at most 64 MiB of HBM per device.

v0:
```python
import math

import jax
import jax.numpy as jnp
from jax import lax
from jax.sharding import PartitionSpec as P

ND = 36
NF = 32
GW = 128


GRAV = 9.81
BASE_FREQ = 0.035
FREQ_RATIO = 1.1
CELL = 5000.0
STEP = 40.0
REFR_LIMIT = 0.5
WIND_RATE = 0.05
DISS_RATE = 0.3
NONLIN_RATE = 0.1


def extended_2(array, sides, width):
    for axis, dim in sides:
        size, length = (lax.axis_size(axis), array.shape[dim])
        up = [(i, (i + 1) % size) for i in range(size)]
        down = [(j, i) for i, j in up]
        last = lax.slice_in_dim(array, length - width, length, axis=dim)
        initial = lax.slice_in_dim(array, 0, width, axis=dim)
        before = lax.ppermute(last, axis, up)
        after = lax.ppermute(initial, axis, down)
        array = jnp.concatenate([before, array, after], axis=dim)
    return array


def bins(kidx):
    band = (kidx // ND).astype(jnp.float32)
    angle_id = (kidx % ND).astype(jnp.float32)
    sigma = 2.0 * math.pi * BASE_FREQ * FREQ_RATIO**band
    theta = 2.0 * math.pi * angle_id / ND
    return (sigma, jnp.cos(theta), jnp.sin(theta))


def wave_terms(sigma, water):
    scaled = sigma * sigma / GRAV * water
    kh = scaled / jnp.tanh(scaled**0.75) ** (2.0 / 3.0)
    decay = jnp.exp(-2.0 * kh)
    denom = 1.0 - decay * decay
    cphase = sigma * water / kh
    cgroup = 0.5 * cphase * (1.0 + 4.0 * kh * decay / denom)
    refr = 2.0 * sigma * decay / denom
    return (cphase, cgroup, refr)


def transport(energy, vel_x, vel_y, e_nb, v_nb, live):
    u_east = 0.5 * (vel_x + v_nb[0])
    f_east = live[0] * (jnp.maximum(u_east, 0.0) * energy + jnp.minimum(u_east, 0.0) * e_nb[0])
    u_west = 0.5 * (v_nb[1] + vel_x)
    f_west = live[1] * (jnp.maximum(u_west, 0.0) * e_nb[1] + jnp.minimum(u_west, 0.0) * energy)
    u_north = 0.5 * (vel_y + v_nb[2])
    f_north = live[2] * (jnp.maximum(u_north, 0.0) * energy + jnp.minimum(u_north, 0.0) * e_nb[2])
    u_south = 0.5 * (v_nb[3] + vel_y)
    f_south = live[3] * (jnp.maximum(u_south, 0.0) * e_nb[3] + jnp.minimum(u_south, 0.0) * energy)
    return energy - STEP / CELL * (f_east - f_west + f_north - f_south)


def sources(energy, water, grad_x, grad_y, wind, mask, interaction):
    total = NF * ND
    width = energy.shape[1]
    sigma, cosine, sine = bins(jnp.arange(total, dtype=jnp.int32))
    cphase, cgroup, refr = wave_terms(sigma[:, None], water[None, :])
    ctheta = -refr * (sine[:, None] * grad_x[None, :] - cosine[:, None] * grad_y[None, :])
    rate = jnp.clip(STEP / (2.0 * math.pi / ND) * ctheta, -REFR_LIMIT, REFR_LIMIT)
    rate3 = rate.reshape(NF, ND, width)
    energy3 = energy.reshape(NF, ND, width)
    face = 0.5 * (rate3 + jnp.roll(rate3, -1, axis=1))
    flow = jnp.maximum(face, 0.0) * energy3 + jnp.minimum(face, 0.0) * jnp.roll(energy3, -1, axis=1)
    refracted = (energy3 - (flow - jnp.roll(flow, 1, axis=1))).reshape(total, width)
    squared = refracted * refracted
    rms = jnp.sqrt(jnp.mean(squared, axis=0) + 1e-06)
    fbar = jnp.sum(sigma[:, None] * squared, axis=0) / (jnp.sum(squared, axis=0) + 1e-06)
    dissipation = DISS_RATE * (sigma[:, None] / fbar[None, :]) ** 2 * (rms / (1.0 + rms))[None, :]
    drive = (wind[0][None, :] * cosine[:, None] + wind[1][None, :] * sine[:, None]) / cphase - 1.0
    gain = WIND_RATE * sigma[:, None] * jnp.maximum(drive, 0.0)
    nonlinear = jnp.dot(
        interaction, squared.astype(jnp.bfloat16), preferred_element_type=jnp.float32
    )
    updated = refracted * (1.0 + gain) + NONLIN_RATE * nonlinear / rms[None, :]
    return mask.astype(jnp.float32)[None, :] * updated / (1.0 + dissipation)


def shifted(extended, tile_cells):
    return [
        extended[..., GW + 1 : GW + 1 + tile_cells],
        extended[..., GW - 1 : GW - 1 + tile_cells],
        extended[..., 2 * GW : 2 * GW + tile_cells],
        extended[..., 0:tile_cells],
    ]


def local(spectrum, depth, currents, winds, sea_mask, neighbours, interaction):
    comp_rows, tile_cells = spectrum.shape
    comp_id = lax.axis_index("comp")
    comp_count = lax.axis_size("comp")
    owned = tile_cells // comp_count
    empty = tile_cells + 2 * GW
    kidx = comp_id * comp_rows + jnp.arange(comp_rows, dtype=jnp.int32)
    sigma, cosine, sine = bins(kidx)
    cphase, cgroup, refr = wave_terms(sigma[:, None], depth[None, :])
    vel_x = cgroup * cosine[:, None] + currents[0][None, :]
    vel_y = cgroup * sine[:, None] + currents[1][None, :]
    stacked = jnp.concatenate([spectrum, vel_x, vel_y, depth[None, :]], axis=0)
    extended = extended_2(stacked, (("tile", 1),), GW)
    e_ext = extended[:comp_rows]
    vx_ext = extended[comp_rows : 2 * comp_rows]
    vy_ext = extended[2 * comp_rows : 3 * comp_rows]
    depth_ext = extended[3 * comp_rows]
    live = (neighbours != empty).astype(jnp.float32)
    e_nb = shifted(e_ext, tile_cells)
    vx_nb = shifted(vx_ext, tile_cells)
    vy_nb = shifted(vy_ext, tile_cells)
    v_nb = [vx_nb[0], vx_nb[1], vy_nb[2], vy_nb[3]]
    own_x = vx_ext[:, GW : GW + tile_cells]
    own_y = vy_ext[:, GW : GW + tile_cells]
    advected = transport(spectrum, own_x, own_y, e_nb, v_nb, live)
    depth_nb = shifted(depth_ext, tile_cells)
    near_depth = [jnp.where(live[j] > 0.0, depth_nb[j], depth) for j in range(4)]
    grad_x = (near_depth[0] - near_depth[1]) / (2.0 * CELL)
    grad_y = (near_depth[2] - near_depth[3]) / (2.0 * CELL)
    gathered = lax.all_to_all(advected, "comp", split_axis=1, concat_axis=0, tiled=True)
    start = comp_id * owned
    water = lax.dynamic_slice_in_dim(depth, start, owned, 0)
    slope_x = lax.dynamic_slice_in_dim(grad_x, start, owned, 0)
    slope_y = lax.dynamic_slice_in_dim(grad_y, start, owned, 0)
    wind = lax.dynamic_slice_in_dim(winds, start, owned, 1)
    mask = lax.dynamic_slice_in_dim(sea_mask, start, owned, 0)
    updated = sources(gathered, water, slope_x, slope_y, wind, mask, interaction)
    return lax.all_to_all(updated, "comp", split_axis=0, concat_axis=1, tiled=True)


def solution(mesh):
    return jax.shard_map(
        local,
        mesh=mesh,
        in_specs=(
            P("comp", "tile"),
            P("tile"),
            P(None, "tile"),
            P(None, "tile"),
            P("tile"),
            P(None, "tile"),
            P(),
        ),
        out_specs=P("comp", "tile"),
        check_vma=False,
    )
```

profile of v0, /device:TPU:0, one launch (start us, length us, event | category | flops | bytes accessed | tf_op | source)
XLA Modules:
  0.0 141.7 jit_solution(15146042968226514190)
XLA Ops:
  0.0 0.1 fusion.136
  0.1 0.9 fusion.147
  1.0 3.5 %multiply_add_fusion.2 = (f32[144,2048]{1,0:T(8,128)S(1)}, f32[144,2048]{1,0:T(8,128)S(1)}) fusion(f32[2048]{0:T(1024)S(1)} %bitcast.44, f32[144]{0:T(256)S(1)} %get-tuple-element.37, f32[144]{0:T(256)S(1)} %get-tuple-element.34, f32[2048]{0:T(1024)} %param.8, f32[144]{0:T(256)S(1)} %get-tuple-element.35, f32[2048]{0:T(1024)S(1)} %bitcast.46, ...), kind=kLoop, calls=%fused_computation.107 | loop fusion | flops 5013504 | bytes 2386176 | tf_op jit(solution)/shard_map/add | solution.py:111
  4.6 2.4 %collective-permute-start = (f32[433,128]{1,0:T(8,128)S(1)}, f32[433,128]{1,0:T(8,128)S(1)}, u32[]{:S(2)}, u32[]{:S(2)}) collective-permute-start(f32[433,128]{1,0:T(8,128)S(1)} %get-tuple-element.16), channel_id=1, source_target_pairs={{1,0},{2,1},{3,2},{0,3},{5,4},{6,5},{7,6},{4,7},{9,8},{10,9},{11,1... | collective-permute-start | bytes 665096 | tf_op jit(solution)/shard_map/ppermute | solution.py:32
  7.1 5.8 %collective-permute-done = f32[433,128]{1,0:T(8,128)S(1)} collective-permute-done((f32[433,128]{1,0:T(8,128)S(1)}, f32[433,128]{1,0:T(8,128)S(1)}, u32[]{:S(2)}, u32[]{:S(2)}) %collective-permute-start) | collective-permute-done | bytes 221728 | tf_op jit(solution)/shard_map/ppermute | solution.py:32
  12.9 1.1 collective-permute-done.1
  14.0 1.4 %pad_maximum_fusion = (f32[433,2176]{1,0:T(8,128)S(1)}, f32[433,2176]{1,0:T(8,128)S(1)}) fusion(f32[433,128]{1,0:T(8,128)S(1)} %collective-permute-done, f32[1,2048]{1,0:T(1,128)S(1)} %bitcast.41, f32[144,2048]{1,0:T(8,128)S(1)} %get-tuple-element.27, f32[144,2048]{1,0:T(8,128)S(1)} %get-tuple-element.26, f32[144,2048]{1,0:T(8,128)S(1)} %copy-done.1, ...), kind=kLoop, calls=%fused_computation | loop fusion | flops 7537664 | bytes 11528192 | tf_op jit(solution)/shard_map/concatenate | solution.py:33
  15.4 4.6 %fusion.64 = f32[144,2048]{1,0:T(8,128)S(1)} fusion(f32[144,2048]{1,0:T(8,128)S(1)} %copy-done.1, f32[433,2176]{1,0:T(8,128)S(1)} %get-tuple-element.15, f32[433,2176]{1,0:T(8,128)S(1)} %get-tuple-element.14, f32[2048]{0:T(1024)S(1)} %bitcast.50, f32[2048]{0:T(1024)S(1)} %bitcast.52, f32[2048]{0:T(1024)S(1)} %bitcast.54, f32[2048]{0:T(1024)S(1)} %bitcast.48, ...), kind=kLoop, calls=%fused_computation.82 | loop fusion | flops 15925248 | bytes 11856128 | tf_op jit(solution)/shard_map/sub | solution.py:65
  20.1 1.1 copy.39
  21.2 5.8 %all-to-all-start = ((f32[144,8,256]{2,0,1:T(8,128)}), f32[144,8,256]{2,0,1:T(8,128)}, u32[]{:S(2)}, u32[]{:S(2)}) async-start(f32[144,8,256]{2,0,1:T(8,128)} %bitcast.37), calls=%async_computation | async-start | bytes 2359296 | tf_op jit(solution)/shard_map/all_to_all | solution.py:131
  27.1 0.8 dynamic-slice_convert_fusion
  27.8 0.8 constant_dynamic-slice_fusion
  28.7 0.1 fusion.124
  28.7 0.1 multiply_multiply_fusion.5
  28.8 0.1 fusion.117
  28.9 0.1 multiply_multiply_fusion.4
  29.0 0.1 fusion.100
  29.1 0.1 pad_maximum_fusion.10
  29.2 1.1 copy-done.2
  30.4 0.4 copy-done.4
  30.7 0.4 copy-done.6
  31.1 0.1 pad_maximum_fusion.11
  31.2 0.1 fusion.148
  31.3 2.8 %fusion.16 = f32[32,36,256]{2,1,0:T(8,128)S(1)} fusion(f32[256]{0:T(256)S(1)} %get-tuple-element.30, f32[32,36]{1,0:T(8,128)S(1)} %get-tuple-element.39, f32[256]{0:T(256)S(1)} %get-tuple-element.29, f32[32,36]{1,0:T(8,128)S(1)} %get-tuple-element.40, f32[256]{0:T(256)S(1)} %get-tuple-element.28, f32[32,36]{1,0:T(8,128)S(1)} %get-tuple-element.38, ...), kind=kLoop, calls=%fused_computation.27 | loop fusion | flops 4128768 | bytes 1201152 | tf_op jit(solution)/shard_map/jit(clip)/min | solution.py:74
  34.1 1.2 slice.182
  35.3 20.1 %all-to-all-done = f32[144,8,256]{2,0,1:T(8,128)} async-done(((f32[144,8,256]{2,0,1:T(8,128)}), f32[144,8,256]{2,0,1:T(8,128)}, u32[]{:S(2)}, u32[]{:S(2)}) %all-to-all-start) | async-done | bytes 1179680 | tf_op jit(solution)/shard_map/all_to_all | solution.py:131
  55.4 2.4 %reshape.228 = f32[32,36,256]{2,1,0:T(8,128)} reshape(f32[8,144,256]{2,1,0:T(8,128)} %bitcast.7) | data formatting | bytes 2359296 | tf_op jit(solution)/shard_map/reshape | solution.py:76
  57.8 1.0 slice.185
  58.8 1.6 %slice.184 = f32[32,35,256]{2,1,0:T(8,128)S(1)} slice(f32[32,36,256]{2,1,0:T(8,128)} %reshape.228), slice={[0:32], [1:36], [0:256]} | slice | bytes 2293760 | tf_op jit(solution)/shard_map/jit(_roll_static)/slice | solution.py:78
  60.4 0.1 copy-done.7
  60.5 0.4 copy-done.8
  60.9 4.5 %multiply_add_fusion = (f32[32,36,256]{2,1,0:T(8,128)S(1)}, f32[32,36,256]{2,1,0:T(8,128)}, f32[32,36,256]{2,1,0:T(8,128)}) fusion(f32[32,36,256]{2,1,0:T(8,128)S(1)} %copy-done.7, f32[256]{0:T(256)S(1)} %get-tuple-element.30, f32[32,36]{1,0:T(8,128)S(1)} %get-tuple-element.39, f32[256]{0:T(256)S(1)} %get-tuple-element.29, ...), kind=kLoop, calls=%fused_computation.31 | loop fusion | flops 6782976 | bytes 7099392 | tf_op jit(solution)/shard_map/add | solution.py:78
  65.4 1.2 pad_maximum_fusion.3
  66.6 2.4 %concatenate.51 = f32[1152,256]{1,0:T(8,128)} reshape(f32[32,36,256]{2,1,0:T(8,128)} %pad_maximum_fusion.3) | data formatting | bytes 2359296 | tf_op jit(solution)/shard_map/jit(_roll_static)/concatenate | solution.py:79
  69.0 2.4 %concatenate.54 = f32[8,144,256]{2,1,0:T(8,128)} reshape(f32[32,36,256]{2,1,0:T(8,128)} %pad_maximum_fusion.3) | data formatting | bytes 2359296 | tf_op jit(solution)/shard_map/jit(_roll_static)/concatenate | solution.py:79
  71.4 2.5 %concatenate.49 = f32[1152,256]{1,0:T(8,128)} reshape(f32[32,36,256]{2,1,0:T(8,128)} %get-tuple-element.9) | data formatting | bytes 2359296 | tf_op jit(solution)/shard_map/jit(_roll_static)/concatenate | solution.py:78
  73.9 2.4 %concatenate.53 = f32[8,144,256]{2,1,0:T(8,128)} reshape(f32[32,36,256]{2,1,0:T(8,128)} %get-tuple-element.9) | data formatting | bytes 2359296 | tf_op jit(solution)/shard_map/jit(_roll_static)/concatenate | solution.py:78
  76.3 2.4 %concatenate.47 = f32[1152,256]{1,0:T(8,128)} reshape(f32[32,36,256]{2,1,0:T(8,128)} %get-tuple-element.8) | data formatting | bytes 2359296 | tf_op jit(solution)/shard_map/jit(_roll_static)/concatenate | solution.py:77
  78.7 2.4 %concatenate.52 = f32[8,144,256]{2,1,0:T(8,128)} reshape(f32[32,36,256]{2,1,0:T(8,128)} %get-tuple-element.8) | data formatting | bytes 2359296 | tf_op jit(solution)/shard_map/jit(_roll_static)/concatenate | solution.py:77
  81.0 2.7 %copy.33 = f32[1152,256]{0,1:T(8,128)} copy(f32[1152,256]{1,0:T(8,128)} %bitcast.8) | data formatting | bytes 2359296 | tf_op jit(solution)/shard_map/reshape | solution.py:76
  83.7 2.7 %copy.32 = f32[1152,256]{0,1:T(8,128)} copy(f32[1152,256]{1,0:T(8,128)} %concatenate.51) | data formatting | bytes 2359296 | tf_op jit(solution)/shard_map/jit(_roll_static)/concatenate | solution.py:79
  86.4 2.7 %copy.31 = f32[1152,256]{0,1:T(8,128)} copy(f32[1152,256]{1,0:T(8,128)} %concatenate.49) | data formatting | bytes 2359296 | tf_op jit(solution)/shard_map/jit(_roll_static)/concatenate | solution.py:78
  89.1 2.8 %copy.29 = f32[1152,256]{0,1:T(8,128)} copy(f32[1152,256]{1,0:T(8,128)} %concatenate.47) | data formatting | bytes 2359296 | tf_op jit(solution)/shard_map/jit(_roll_static)/concatenate | solution.py:77
  91.8 5.0 %multiply_reduce_fusion = (f32[256]{0:T(256)S(1)}, f32[256]{0:T(256)S(1)}) fusion(f32[8,144]{1,0:T(8,128)S(1)} %get-tuple-element.45, f32[8,144,256]{2,1,0:T(8,128)} %concatenate.54, f32[8,144,256]{2,1,0:T(8,128)} %concatenate.53, f32[8,144,256]{2,1,0:T(8,128)} %concatenate.52, f32[256]{0:T(256)S(1)} %get-tuple-element.30, ...), kind=kLoop, calls=%fused_computation.102 | loop fusion | flops 7962112 | bytes 4746752 | tf_op jit(solution)/shard_map/reduce_sum | solution.py:82
  96.9 8.5 %fusion.4 = f32[1152,256]{0,1:T(8,128)} fusion(bf16[1152,1152]{1,0:T(8,128)(2,1)S(1)} %copy-done, f32[1152,256]{0,1:T(8,128)S(1)} %copy-done.9, f32[1152,256]{0,1:T(8,128)S(1)} %copy-done.10, f32[1152,256]{0,1:T(8,128)S(1)} %copy-done.11, f32[1152,256]{0,1:T(8,128)S(1)} %copy-done.12, f32[256]{0:T(256)S(1)} %get-tuple-element.32, ...), kind=kOutput, calls=%fused_computation.7 | convolution fusion | flops 699531264 | bytes 8589312 | tf_op jit(solution)/shard_map/dot_general | solution.py:86
  105.4 2.7 %copy.34 = f32[1152,256]{1,0:T(8,128)} copy(f32[1152,256]{0,1:T(8,128)} %fusion.4) | data formatting | bytes 2359296 | tf_op jit(solution)/shard_map/div | solution.py:90
  108.0 32.5 %all_to_all.35 = f32[8,144,256]{2,1,0:T(8,128)S(1)} all-to-all(f32[8,144,256]{2,1,0:T(8,128)} %bitcast.38), channel_id=1, replica_groups=mesh['comp'=8,'tile'=4] {'comp'}, dimensions={0} | all-to-all | bytes 2359296 | tf_op jit(solution)/shard_map/all_to_all | solution.py:139
  140.5 1.1 copy.37
  (36 shorter events, 0.3 us)
Async XLA Ops:
  0.0 96.9 %copy-start = (bf16[1152,1152]{1,0:T(8,128)(2,1)S(1)}, bf16[1152,1152]{1,0:T(8,128)(2,1)}, u32[]{:S(2)}) copy-start(bf16[1152,1152]{1,0:T(8,128)(2,1)} %param.13) | copy-start | bytes 7962628
  1.0 3.6 %copy-start.1 = (f32[144,2048]{1,0:T(8,128)S(1)}, f32[144,2048]{1,0:T(8,128)}, u32[]{:S(2)}) copy-start(f32[144,2048]{1,0:T(8,128)} %param.7) | copy-start | bytes 3538948
  1.0 3.6 %copy-start.13 = (f32[2048]{0:T(1024)S(1)}, f32[2048]{0:T(1024)}, u32[]{:S(2)}) copy-start(f32[2048]{0:T(1024)} %param.8) | copy-start | bytes 24580
  4.5 9.5 %copy-start.3 = (f32[144,2048]{1,0:T(8,128)}, f32[144,2048]{1,0:T(8,128)S(1)}, u32[]{:S(2)}) copy-start(f32[144,2048]{1,0:T(8,128)S(1)} %get-tuple-element.26) | copy-start | bytes 3538948
  4.6 9.4 %copy-start.5 = (f32[144,2048]{1,0:T(8,128)}, f32[144,2048]{1,0:T(8,128)S(1)}, u32[]{:S(2)}) copy-start(f32[144,2048]{1,0:T(8,128)S(1)} %get-tuple-element.27) | copy-start | bytes 3538948
  4.6 2.5 %copy-start.14 = (s32[4,2048]{1,0:T(4,128)S(1)}, s32[4,2048]{1,0:T(4,128)}, u32[]{:S(2)}) copy-start(s32[4,2048]{1,0:T(4,128)} %param.12) | copy-start | bytes 98308
  4.6 8.3 %collective-permute-start = (f32[433,128]{1,0:T(8,128)S(1)}, f32[433,128]{1,0:T(8,128)S(1)}, u32[]{:S(2)}, u32[]{:S(2)}) collective-permute-start(f32[433,128]{1,0:T(8,128)S(1)} %get-tuple-element.16), channel_id=1, source_target_pairs={{1,0},{2,1},{3,2},{0,3},{5,4},{6,5},{7,6},{4,7},{9,8},{10,9},{11,1... | collective-permute-start | bytes 665096 | tf_op jit(solution)/shard_map/ppermute | solution.py:32
  7.1 6.9 %collective-permute-start.1 = (f32[433,128]{1,0:T(8,128)S(1)}, f32[433,128]{1,0:T(8,128)S(1)}, u32[]{:S(2)}, u32[]{:S(2)}) collective-permute-start(f32[433,128]{1,0:T(8,128)S(1)} %get-tuple-element.17), channel_id=1, source_target_pairs={{0,1},{1,2},{2,3},{3,0},{4,5},{5,6},{6,7},{7,4},{8,9},{9,10},{10,1... | collective-permute-start | bytes 665096 | tf_op jit(solution)/shard_map/ppermute | solution.py:31
  21.2 34.2 %all-to-all-start = ((f32[144,8,256]{2,0,1:T(8,128)}), f32[144,8,256]{2,0,1:T(8,128)}, u32[]{:S(2)}, u32[]{:S(2)}) async-start(f32[144,8,256]{2,0,1:T(8,128)} %bitcast.37), calls=%async_computation | async-start | bytes 2359296 | tf_op jit(solution)/shard_map/all_to_all | solution.py:131
  29.1 1.3 copy-start.2
  29.1 1.6 %copy-start.4 = (f32[144,2048]{1,0:T(8,128)S(1)}, f32[144,2048]{1,0:T(8,128)}, u32[]{:S(2)}) copy-start(f32[144,2048]{1,0:T(8,128)} %copy-done.3) | copy-start | bytes 3538948
  29.1 2.0 %copy-start.6 = (f32[144,2048]{1,0:T(8,128)S(1)}, f32[144,2048]{1,0:T(8,128)}, u32[]{:S(2)}) copy-start(f32[144,2048]{1,0:T(8,128)} %copy-done.5) | copy-start | bytes 3538948
  58.8 1.7 %copy-start.7 = (f32[32,36,256]{2,1,0:T(8,128)S(1)}, f32[32,36,256]{2,1,0:T(8,128)}, u32[]{:S(2)}) copy-start(f32[32,36,256]{2,1,0:T(8,128)} %reshape.228) | copy-start | bytes 3538948
  58.8 2.1 %copy-start.8 = (f32[32,35,256]{2,1,0:T(8,128)S(1)}, f32[32,35,256]{2,1,0:T(8,128)}, u32[]{:S(2)}) copy-start(f32[32,35,256]{2,1,0:T(8,128)} %slice.182) | copy-start | bytes 3440644
  91.8 5.0 %copy-start.9 = (f32[1152,256]{0,1:T(8,128)S(1)}, f32[1152,256]{0,1:T(8,128)}, u32[]{:S(2)}) copy-start(f32[1152,256]{0,1:T(8,128)} %copy.33) | copy-start | bytes 3538948
  91.8 5.0 %copy-start.10 = (f32[1152,256]{0,1:T(8,128)S(1)}, f32[1152,256]{0,1:T(8,128)}, u32[]{:S(2)}) copy-start(f32[1152,256]{0,1:T(8,128)} %copy.32) | copy-start | bytes 3538948
  91.8 5.0 %copy-start.11 = (f32[1152,256]{0,1:T(8,128)S(1)}, f32[1152,256]{0,1:T(8,128)}, u32[]{:S(2)}) copy-start(f32[1152,256]{0,1:T(8,128)} %copy.31) | copy-start | bytes 3538948
  91.8 5.1 %copy-start.12 = (f32[1152,256]{0,1:T(8,128)S(1)}, f32[1152,256]{0,1:T(8,128)}, u32[]{:S(2)}) copy-start(f32[1152,256]{0,1:T(8,128)} %copy.29) | copy-start | bytes 3538948
where the time goes:
time: 142 us
  local copies, waits for them, and re-layouts  40.5 us (29%)
  blocking collectives  32.5 us (23%)
  waiting for transfers between devices  27 us (19%)
  other arithmetic  24.7 us (17%)
  matrix products  8.46 us (6%)
  starting transfers between devices  8.27 us (6%)
    all_to_all x1, blocking collectives, local(): lax.all_to_all(updated, 'comp', split_axis=0, concat_axis=1, tiled=True)  32.5 us
    all_to_all x1, waiting for transfers between devices, local(): lax.all_to_all(advected, 'comp', split_axis=1, concat_axis=0, tiled=True)  20.1 us
    dot_general x1, matrix products, sources(): jnp.dot(interaction, squared.astype(jnp.bfloat16), preferred_element_type...  8.46 us
    concatenate x3, local copies, waits for them, and re-layouts, sources(): face = 0.5 * (rate3 + jnp.roll(rate3, -1, axis=1))  7.55 us
    concatenate x3, local copies, waits for them, and re-layouts, sources(): jnp.roll(energy3, -1, axis=1)  7.55 us
    concatenate x3, local copies, waits for them, and re-layouts, sources(): jnp.roll(flow, 1, axis=1)  7.48 us
    all_to_all x1, starting transfers between devices, local(): lax.all_to_all(advected, 'comp', split_axis=1, concat_axis=0, tiled=True)  5.84 us
    ppermute x1, waiting for transfers between devices, extended_2(): after = lax.ppermute(initial, axis, down)  5.8 us
  transfers between devices with their start and end apart: 3, of which 3 were waited for; matrix products, arithmetic and copies ran while one was open for 4% of the time, Pallas kernels for 0%

commit v1 on v0

--- a/solution.py
+++ b/solution.py
@@ -1,8 +1,12 @@
+import functools
 import math
 
 import jax
 import jax.numpy as jnp
+import numpy as np
 from jax import lax
+from jax.experimental import pallas as pl
+from jax.experimental.pallas import tpu as pltpu
 from jax.sharding import PartitionSpec as P
 
 ND = 36
@@ -139,9 +143,392 @@
     return lax.all_to_all(updated, "comp", split_axis=0, concat_axis=1, tiled=True)
 
 
+def tables(comps, rows):
+    angle = 2.0 * math.pi * (np.arange(rows) % ND) / ND
+    sigma = 2.0 * math.pi * BASE_FREQ * FREQ_RATIO ** np.arange(NF, dtype=np.float64)
+    bands = rows // ND
+    by_comp = np.ones((comps, 8))
+    by_comp[:, :bands] = sigma.reshape(comps, bands)
+    lanes = np.ones((GW,))
+    return (
+        np.float32(np.cos(angle)[:, None] * lanes),
+        np.float32(np.sin(angle)[:, None] * lanes),
+        np.float32(by_comp[:, :, None] * lanes),
+    )
+
+
+def fits(comps, rows, cells):
+    return rows % ND == 0 and rows % 16 == 0 and rows // ND <= 8 and cells == 2 * comps * GW and comps % 2 == 0
+
+
+def wave_kernel(
+    comps, tiles, rows,
+    spec, depth, currents, winds, mask, neighbours, cosine, sine, sigmas, inter,
+    out,
+    field, cell, group, refr, slow, matrix, refracted, sq_send, sq_recv, nl_send, nl_recv, d_send, d_recv, half,
+    in_sem, mat_sem, out_sem, halo_send, halo_recv, s1, r1, s2, r2, s3, r3,
+):
+    grid_rows = 2 * comps
+    bands = rows // ND
+    empty = grid_rows * GW + 2 * GW
+    me = lax.axis_index("comp")
+    tile = lax.axis_index("tile")
+    later = lax.rem(tile + 1, tiles)
+    earlier = lax.rem(tile + tiles - 1, tiles)
+    f32 = jnp.float32
+
+    barrier = pltpu.get_barrier_semaphore()
+    for off in range(1, comps):
+        pl.semaphore_signal(
+            barrier, inc=1, device_id={"comp": lax.rem(me + off, comps)}, device_id_type=pl.DeviceIdType.MESH
+        )
+    for side in (later, earlier):
+        pl.semaphore_signal(barrier, inc=1, device_id={"tile": side}, device_id_type=pl.DeviceIdType.MESH)
+
+    def load(g):
+        return pltpu.make_async_copy(spec.at[:, g * GW : (g + 1) * GW], field.at[g + 1], in_sem.at[g])
+
+    for g in range(grid_rows):
+        load(g).start()
+    matrix_copy = pltpu.make_async_copy(inter, matrix, mat_sem)
+    matrix_copy.start()
+
+    sigma = sigmas[me]
+
+    def waves(row):
+        water = cell[row, 0:1, :]
+        scaled = sigma * sigma * (1.0 / GRAV) * water
+        kh = scaled * jnp.exp((-2.0 / 3.0) * jnp.log(jnp.tanh(jnp.sqrt(scaled * jnp.sqrt(scaled)))))
+        decay = jnp.exp(-2.0 * kh)
+        denom = 1.0 - decay * decay
+        cphase = sigma * water / kh
+        group[row] = 0.5 * cphase * (1.0 + 4.0 * kh * decay / denom)
+        refr[row] = 2.0 * sigma * decay / denom
+        slow[row] = kh / (sigma * water)
+
+    for g in range(grid_rows):
+        lanes = slice(g * GW, (g + 1) * GW)
+        cell[g + 1, 0:1, :] = depth[:, lanes]
+        cell[g + 1, 1:3, :] = currents[:, lanes]
+        cell[g + 1, 3:5, :] = winds[:, lanes]
+        cell[g + 1, 5:6, :] = mask[:, lanes].astype(f32)
+        cell[g + 1, 6:8, :] = jnp.zeros((2, GW), f32)
+    for g in range(grid_rows):
+        waves(g + 1)
+
+    for g in range(grid_rows):
+        load(g).wait()
+    pl.semaphore_wait(barrier, comps + 1)
+
+    def halo(buffer, which):
+        return (
+            pltpu.make_async_remote_copy(
+                src_ref=buffer.at[1], dst_ref=buffer.at[grid_rows + 1],
+                send_sem=halo_send.at[which], recv_sem=halo_recv.at[which],
+                device_id={"tile": earlier}, device_id_type=pl.DeviceIdType.MESH,
+            ),
+            pltpu.make_async_remote_copy(
+                src_ref=buffer.at[grid_rows], dst_ref=buffer.at[0],
+                send_sem=halo_send.at[which + 1], recv_sem=halo_recv.at[which + 1],
+                device_id={"tile": later}, device_id_type=pl.DeviceIdType.MESH,
+            ),
+        )
+
+    halos = halo(cell, 0) + halo(field, 2)
+    for copy in halos:
+        copy.start()
+
+    row_of = lax.broadcasted_iota(jnp.int32, (rows, GW), 0)
+    last_dir = functools.reduce(jnp.logical_or, [row_of == ND * b + ND - 1 for b in range(bands)])
+    first_dir = functools.reduce(jnp.logical_or, [row_of == ND * b for b in range(bands)])
+    lane = lax.broadcasted_iota(jnp.int32, (rows, GW), 1)
+    lane8 = lax.broadcasted_iota(jnp.int32, (8, GW), 1)
+    sub8 = lax.broadcasted_iota(jnp.int32, (8, GW), 0)
+
+    def spread(c):
+        by_band = [jnp.broadcast_to(c[b : b + 1], (8, GW)) for b in range(bands)]
+        slabs = []
+        for r in range(rows // 8):
+            low, high = 8 * r // ND, (8 * r + 7) // ND
+            if low == high:
+                slabs.append(by_band[low])
+            else:
+                slabs.append(jnp.where(sub8 < ND * high - 8 * r, by_band[low], by_band[high]))
+        return jnp.concatenate(slabs, axis=0)
+
+    def along(x, following, lanes):
+        return jnp.where(lanes == GW - 1, pltpu.roll(following, GW - 1, 1), pltpu.roll(x, GW - 1, 1))
+
+    def back(x, preceding, lanes):
+        return jnp.where(lanes == 0, pltpu.roll(preceding, 1, 1), pltpu.roll(x, 1, 1))
+
+    def next_dir(x):
+        return jnp.where(last_dir, pltpu.roll(x, ND - 1, 0), pltpu.roll(x, rows - 1, 0))
+
+    def prev_dir(x):
+        return jnp.where(first_dir, pltpu.roll(x, rows - ND + 1, 0), pltpu.roll(x, 1, 0))
+
+    def grid_row(h, who):
+        if h == 0:
+            return comps // 2 + who
+        return who + comps * (who // (comps // 2))
+
+    def advance(g):
+        e, e_n, e_s = field[g + 1], field[g + 2], field[g]
+        nb = neighbours[:, pl.ds(pl.multiple_of(g * GW, GW), GW)]
+        live = (nb != empty).astype(f32)
+        c, c_n, c_s = cell[g + 1], cell[g + 2], cell[g]
+        v, v_n, v_s = group[g + 1], group[g + 2], group[g]
+        c_e, c_w = along(c, c_n, lane8), back(c, c_s, lane8)
+        v_e, v_w = along(v, v_n, lane8), back(v, v_s, lane8)
+        cos_k, sin_k = cosine[...], sine[...]
+
+        def face(j, direction, axis, v_j, c_j):
+            weight = (0.5 * STEP / CELL) * live[j : j + 1]
+            wave = weight * (v + v_j)
+            flow = weight * (c[axis : axis + 1] + c_j[axis : axis + 1])
+            return direction * spread(wave) + flow
+
+        u_e = face(0, cos_k, 1, v_e, c_e)
+        u_w = face(1, cos_k, 1, v_w, c_w)
+        u_n = face(2, sin_k, 2, v_n, c_n)
+        u_s = face(3, sin_k, 2, v_s, c_s)
+        f_e = jnp.maximum(u_e, 0.0) * e + jnp.minimum(u_e, 0.0) * along(e, e_n, lane)
+        f_w = jnp.maximum(u_w, 0.0) * back(e, e_s, lane) + jnp.minimum(u_w, 0.0) * e
+        f_n = jnp.maximum(u_n, 0.0) * e + jnp.minimum(u_n, 0.0) * e_n
+        f_s = jnp.maximum(u_s, 0.0) * e_s + jnp.minimum(u_s, 0.0) * e
+        adv = e - (f_e - f_w + f_n - f_s)
+
+        h = c[0:1]
+        near = [jnp.where(live[j : j + 1] > 0.0, x[0:1], h) for j, x in enumerate((c_e, c_w, c_n, c_s))]
+        scale = (0.5 * STEP / (2.0 * math.pi / ND) / (2.0 * CELL)) * refr[g + 1]
+        from_x = scale * (near[1] - near[0])
+        from_y = scale * (near[2] - near[3])
+        rate = jnp.clip(sin_k * spread(from_x) + cos_k * spread(from_y), -0.5 * REFR_LIMIT, 0.5 * REFR_LIMIT)
+        m = rate + next_dir(rate)
+        flow = jnp.maximum(m, 0.0) * adv + jnp.minimum(m, 0.0) * next_dir(adv)
+        return adv - (flow - prev_dir(flow))
+
+    def peer(s):
+        return lax.rem(me + comps // 2 + s // 2 - (s % 2) * (2 * (s // 2) + 1) + comps, comps)
+
+    def sender(s):
+        return lax.rem(me + 2 * comps - (comps // 2 + s // 2 - (s % 2) * (2 * (s // 2) + 1)), comps)
+
+    def first(h, who):
+        return pltpu.make_async_remote_copy(
+            src_ref=sq_send.at[h, who], dst_ref=sq_recv.at[h, me],
+            send_sem=s1.at[h, who], recv_sem=r1.at[h, me],
+            device_id={"comp": who}, device_id_type=pl.DeviceIdType.MESH,
+        )
+
+    def first_arrival(h, who):
+        return pltpu.make_async_remote_copy(
+            src_ref=sq_send.at[h, who], dst_ref=sq_recv.at[h, who],
+            send_sem=s1.at[h, who], recv_sem=r1.at[h, who],
+            device_id={"comp": who}, device_id_type=pl.DeviceIdType.MESH,
+        )
+
+    def second(h, who):
+        return pltpu.make_async_remote_copy(
+            src_ref=nl_send.at[h, who], dst_ref=nl_recv.at[h, me],
+            send_sem=s2.at[h, who], recv_sem=r2.at[h, me],
+            device_id={"comp": who}, device_id_type=pl.DeviceIdType.MESH,
+        )
+
+    def second_arrival(h, who):
+        return pltpu.make_async_remote_copy(
+            src_ref=nl_send.at[h, who], dst_ref=nl_recv.at[h, who],
+            send_sem=s2.at[h, who], recv_sem=r2.at[h, who],
+            device_id={"comp": who}, device_id_type=pl.DeviceIdType.MESH,
+        )
+
+    def third(h, who):
+        return pltpu.make_async_remote_copy(
+            src_ref=d_send.at[h], dst_ref=d_recv.at[h, me],
+            send_sem=s3.at[h, who], recv_sem=r3.at[h, me],
+            device_id={"comp": who}, device_id_type=pl.DeviceIdType.MESH,
+        )
+
+    def third_arrival(h, who):
+        return pltpu.make_async_remote_copy(
+            src_ref=d_send.at[h], dst_ref=d_recv.at[h, who],
+            send_sem=s3.at[h, who], recv_sem=r3.at[h, who],
+            device_id={"comp": who}, device_id_type=pl.DeviceIdType.MESH,
+        )
+
+    def store(who, g, h, target):
+        r = advance(g)
+        refracted[g] = r
+        target[...] = r * r
+
+    for h in range(2):
+        if h == 1:
+            for copy in halos:
+                copy.wait()
+            waves(0)
+            waves(grid_rows + 1)
+
+        def send(s, carry):
+            who = peer(s)
+            store(who, grid_row(h, who), h, sq_send.at[h, who])
+            first(h, who).start()
+            return carry
+
+        lax.fori_loop(0, comps - 1, send, 0)
+        store(me, grid_row(h, me), h, sq_recv.at[h, me])
+
+    matrix_copy.wait()
+    for h in range(2):
+        def arrive(s, carry):
+            first_arrival(h, sender(s)).wait_recv()
+            return carry
+
+        lax.fori_loop(0, comps - 1, arrive, 0)
+
+        def add(who, sums):
+            square = sq_recv[h, who]
+            half[pl.ds(pl.multiple_of(who * rows, 16), rows), :] = square.astype(jnp.bfloat16)
+            weighted = spread(sigmas[who]) * square
+            return (
+                sums[0] + jnp.sum(square.reshape(rows // 8, 8, GW), axis=0),
+                sums[1] + jnp.sum(weighted.reshape(rows // 8, 8, GW), axis=0),
+            )
+
+        zero = jnp.zeros((8, GW), f32)
+        total, moment = lax.fori_loop(0, comps, add, (zero, zero))
+        total = jnp.sum(total, axis=0, keepdims=True)
+        moment = jnp.sum(moment, axis=0, keepdims=True)
+        rms = jnp.sqrt(total * (1.0 / (NF * ND)) + 1e-06)
+        inverse = (total + 1e-06) / moment
+        loss = DISS_RATE * inverse * inverse * (rms / (1.0 + rms))
+        d_send[h] = loss
+        d_recv[h, me] = loss
+        scale = NONLIN_RATE / rms
+
+        def product(who):
+            part = matrix[pl.ds(pl.multiple_of(who * rows, 16), rows), :]
+            return scale * jnp.dot(part, half[...], preferred_element_type=f32)
+
+        def reply(s, carry):
+            who = peer(s)
+            nl_send[h, who] = product(who)
+            second(h, who).start()
+            third(h, who).start()
+            return carry
+
+        lax.fori_loop(0, comps - 1, reply, 0)
+        nl_recv[h, me] = product(me)
+
+    def finish(h, who):
+        g = grid_row(h, who)
+        c = cell[g + 1]
+        keep = c[5:6] / (1.0 + sigma * sigma * d_recv[h, who])
+        rate = WIND_RATE * sigma
+        growth = rate * slow[g + 1]
+        drive = cosine[...] * spread(growth * c[3:4]) + sine[...] * spread(growth * c[4:5])
+        gain = jnp.maximum(drive - spread(rate), 0.0)
+        r = refracted[g]
+        refracted[g] = spread(keep) * (r * (1.0 + gain) + nl_recv[h, who])
+        pltpu.make_async_copy(
+            refracted.at[g], out.at[:, pl.ds(pl.multiple_of(g * GW, GW), GW)], out_sem.at[h, who]
+        ).start()
+
+    for h in range(2):
+        finish(h, me)
+
+        def complete(s, carry):
+            who = sender(comps - 2 - s)
+            second_arrival(h, who).wait_recv()
+            third_arrival(h, who).wait_recv()
+            finish(h, who)
+            return carry
+
+        lax.fori_loop(0, comps - 1, complete, 0)
+
+    for h in range(2):
+        def drain(s, carry):
+            who = peer(s)
+            first(h, who).wait_send()
+            second(h, who).wait_send()
+            third(h, who).wait_send()
+            return carry
+
+        lax.fori_loop(0, comps - 1, drain, 0)
+
+        def written(who, carry):
+            g = grid_row(h, who)
+            pltpu.make_async_copy(
+                refracted.at[g], out.at[:, pl.ds(pl.multiple_of(g * GW, GW), GW)], out_sem.at[h, who]
+            ).wait()
+            return carry
+
+        lax.fori_loop(0, comps, written, 0)
+
+
+def fused(spectrum, depth, currents, winds, sea_mask, neighbours, interaction):
+    rows, cells = spectrum.shape
+    comps, tiles = lax.axis_size("comp"), lax.axis_size("tile")
+    grid_rows = cells // GW
+    cosine, sine, sigmas = tables(comps, rows)
+    vmem = pl.BlockSpec(memory_space=pltpu.VMEM)
+    hbm = pl.BlockSpec(memory_space=pl.ANY)
+    f32 = jnp.float32
+    dma = pltpu.SemaphoreType.DMA
+    return pl.pallas_call(
+        functools.partial(wave_kernel, comps, tiles, rows),
+        out_shape=jax.ShapeDtypeStruct((rows, cells), f32),
+        in_specs=[hbm] + [vmem] * 8 + [hbm],
+        out_specs=hbm,
+        scratch_shapes=[
+            pltpu.VMEM((grid_rows + 2, rows, GW), f32),
+            pltpu.VMEM((grid_rows + 2, 8, GW), f32),
+            pltpu.VMEM((grid_rows + 2, 8, GW), f32),
+            pltpu.VMEM((grid_rows + 2, 8, GW), f32),
+            pltpu.VMEM((grid_rows + 2, 8, GW), f32),
+            pltpu.VMEM(interaction.shape, jnp.bfloat16),
+            pltpu.VMEM((grid_rows, rows, GW), f32),
+            pltpu.VMEM((2, comps, rows, GW), f32),
+            pltpu.VMEM((2, comps, rows, GW), f32),
+            pltpu.VMEM((2, comps, rows, GW), f32),
+            pltpu.VMEM((2, comps, rows, GW), f32),
+            pltpu.VMEM((2, 1, GW), f32),
+            pltpu.VMEM((2, comps, 1, GW), f32),
+            pltpu.VMEM((comps * rows, GW), jnp.bfloat16),
+            dma((grid_rows,)),
+            dma,
+            dma((2, comps)),
+            dma((4,)),
+            dma((4,)),
+            dma((2, comps)),
+            dma((2, comps)),
+            dma((2, comps)),
+            dma((2, comps)),
+            dma((2, comps)),
+            dma((2, comps)),
+        ],
+        compiler_params=pltpu.CompilerParams(
+            collective_id=0, has_side_effects=True, vmem_limit_bytes=32 * 1024 * 1024
+        ),
+        cost_estimate=pl.CostEstimate(
+            flops=2 * cells // comps * (comps * rows) ** 2, bytes_accessed=8 * rows * cells, transcendentals=0
+        ),
+    )(
+        spectrum, depth.reshape(1, cells), currents, winds, sea_mask.reshape(1, cells), neighbours,
+        jnp.asarray(cosine), jnp.asarray(sine), jnp.asarray(sigmas), interaction,
+    )
+
+
+def step(spectrum, *rest):
+    rows, cells = spectrum.shape
+    if fits(lax.axis_size("comp"), rows, cells):
+        return fused(spectrum, *rest)
+    return local(spectrum, *rest)
+
+
 def solution(mesh):
     return jax.shard_map(
-        local,
+        step,
         mesh=mesh,
         in_specs=(
             P("comp", "tile"),

time: 142 us -> 68.5 us (0.48)
  Pallas kernels: 0 us -> 57.8 us
  blocking collectives: 32.5 us -> 0 us
  local copies, waits for them, and re-layouts: 40.5 us -> 10.1 us
  waiting for transfers between devices: 27 us -> 0 us
  other arithmetic: 24.7 us -> 0 us
  matrix products: 8.46 us -> 0 us
  starting transfers between devices: 8.27 us -> 0 us
    pallas_call x0 -> x1, Pallas kernels: none -> 57.8 us  [fused(): pl.pallas_call(functools.partial(wave_kernel, comps, tiles, rows), out_sh...]
    all_to_all x1 -> x0, blocking collectives: 32.5 us -> none  [local(): lax.all_to_all(updated, 'comp', split_axis=0, concat_axis=1, tiled=True)]
    concatenate x9 -> x0, local copies, waits for them, and re-layouts: 22.6 us -> none  [the longest x3 7.55 us: sources(): face = 0.5 * (rate3 + jnp.roll(rate3, -1, axis=1))]
    all_to_all x1 -> x0, waiting for transfers between devices: 20.1 us -> none  [local(): lax.all_to_all(advected, 'comp', split_axis=1, concat_axis=0, tiled=True)]
    dot_general x1 -> x0, matrix products: 8.46 us -> none  [sources(): jnp.dot(interaction, squared.astype(jnp.bfloat16), preferred_element_type...]
    add x2 -> x0, other arithmetic: 8 us -> none  [the longest x1 4.48 us: sources(): jnp.maximum(face, 0.0) * energy3]
    unnamed x30 -> x21, local copies, waits for them, and re-layouts: 2.43 us -> 10.1 us
    ppermute x2 -> x0, waiting for transfers between devices: 6.88 us -> none  [the longest x1 5.8 us: extended_2(): after = lax.ppermute(initial, axis, down)]
  transfers between devices with their start and end apart: 3 -> 0, of which waited for: 3 -> 0; matrix products, arithmetic and copies ran while one was open for 4% -> 0% of each run, Pallas kernels for 0% -> 0%
where the time goes in v1:
time: 68.5 us; the launch traced here: 67.9 us
  Pallas kernels  57.8 us (84%)
  local copies, waits for them, and re-layouts  10.1 us (15%)
    pallas_call x1, Pallas kernels, fused(): pl.pallas_call(functools.partial(wave_kernel, comps, tiles, rows), out_sh...  57.8 us
    unnamed x21, local copies, waits for them, and re-layouts  10.1 us

profile of v1, /device:TPU:0, one launch (start us, length us, event | category | flops | bytes accessed | tf_op | source)
XLA Modules:
  0.0 67.9 jit_solution(13863999377965429038)
XLA Ops:
  0.0 0.0 copy-start
  0.0 1.7 %copy-done = bf16[1152,1152]{1,0:T(8,128)(2,1)S(1)} copy-done((bf16[1152,1152]{1,0:T(8,128)(2,1)S(1)}, bf16[1152,1152]{1,0:T(8,128)(2,1)}, u32[]{:S(2)}) %copy-start) | copy-done | bytes 2654232
  1.8 0.0 copy-start.1
  1.8 1.3 %copy-done.1 = f32[144,2048]{1,0:T(8,128)S(1)} copy-done((f32[144,2048]{1,0:T(8,128)S(1)}, f32[144,2048]{1,0:T(8,128)}, u32[]{:S(2)}) %copy-start.1) | copy-done | bytes 1179672
  3.0 0.0 copy-start.2
  3.0 0.9 %copy-done.2 = f32[144,128]{1,0:T(8,128)S(1)} copy-done((f32[144,128]{1,0:T(8,128)S(1)}, f32[144,128]{1,0:T(8,128)}, u32[]{:S(2)}) %copy-start.2) | copy-done | bytes 73752
  3.9 0.0 copy-start.3
  3.9 0.9 %copy-done.3 = f32[144,128]{1,0:T(8,128)S(1)} copy-done((f32[144,128]{1,0:T(8,128)S(1)}, f32[144,128]{1,0:T(8,128)}, u32[]{:S(2)}) %copy-start.3) | copy-done | bytes 73752
  4.8 0.0 copy-start.4
  4.8 0.8 %copy-done.4 = s32[4,2048]{1,0:T(4,128)S(1)} copy-done((s32[4,2048]{1,0:T(4,128)S(1)}, s32[4,2048]{1,0:T(4,128)}, u32[]{:S(2)}) %copy-start.4) | copy-done | bytes 32792
  5.5 0.0 copy-start.5
  5.6 0.8 %copy-done.5 = f32[8,8,128]{2,1,0:T(8,128)S(1)} copy-done((f32[8,8,128]{2,1,0:T(8,128)S(1)}, f32[8,8,128]{2,1,0:T(8,128)}, u32[]{:S(2)}) %copy-start.5) | copy-done | bytes 32792
  6.3 0.0 copy-start.6
  6.3 0.7 %copy-done.6 = f32[2,2048]{1,0:T(2,128)S(1)} copy-done((f32[2,2048]{1,0:T(2,128)S(1)}, f32[2,2048]{1,0:T(2,128)}, u32[]{:S(2)}) %copy-start.6) | copy-done | bytes 16408
  7.0 0.0 copy-start.7
  7.0 0.7 %copy-done.7 = f32[2,2048]{1,0:T(2,128)S(1)} copy-done((f32[2,2048]{1,0:T(2,128)S(1)}, f32[2,2048]{1,0:T(2,128)}, u32[]{:S(2)}) %copy-start.7) | copy-done | bytes 16408
  7.7 0.0 copy-start.8
  7.7 0.7 %copy-done.8 = f32[2048]{0:T(1024)S(1)} copy-done((f32[2048]{0:T(1024)S(1)}, f32[2048]{0:T(1024)}, u32[]{:S(2)}) %copy-start.8) | copy-done | bytes 8216
  8.4 0.0 copy-start.9
  8.4 0.7 %copy-done.9 = s32[2048]{0:T(1024)S(1)} copy-done((s32[2048]{0:T(1024)S(1)}, s32[2048]{0:T(1024)}, u32[]{:S(2)}) %copy-start.9) | copy-done | bytes 8216
  9.1 57.8 %shard_map.100 = f32[144,2048]{1,0:T(8,128)S(1)} custom-call(f32[144,2048]{1,0:T(8,128)S(1)} %copy-done.1, f32[1,2048]{1,0:T(1,128)S(1)} %bitcast.2, f32[2,2048]{1,0:T(2,128)S(1)} %copy-done.6, f32[2,2048]{1,0:T(2,128)S(1)} %copy-done.7, s32[1,2048]{1,0:T(1,128)S(1)} %bitcast.3, s32[4,2048]{1,0:T(4,128)S(1)} %copy-done.4, f32[144,128]{1,0:T(8,128)S(1)} %copy-done.3, ...), custom_call_target="tpu_custom_call" | custom-call | flops 679477248 | bytes 2359296 | tf_op jit(solution)/shard_map/pallas_call | solution.py:478
  66.9 1.0 %copy.12 = f32[144,2048]{1,0:T(8,128)} copy(f32[144,2048]{1,0:T(8,128)S(1)} %shard_map.100) | data formatting | bytes 2359296
Async XLA Ops:
  0.0 1.7 %copy-start = (bf16[1152,1152]{1,0:T(8,128)(2,1)S(1)}, bf16[1152,1152]{1,0:T(8,128)(2,1)}, u32[]{:S(2)}) copy-start(bf16[1152,1152]{1,0:T(8,128)(2,1)} %inter.1) | copy-start | bytes 7962628
  1.8 1.3 %copy-start.1 = (f32[144,2048]{1,0:T(8,128)S(1)}, f32[144,2048]{1,0:T(8,128)}, u32[]{:S(2)}) copy-start(f32[144,2048]{1,0:T(8,128)} %spec.1) | copy-start | bytes 3538948
  3.0 0.9 %copy-start.2 = (f32[144,128]{1,0:T(8,128)S(1)}, f32[144,128]{1,0:T(8,128)}, u32[]{:S(2)}) copy-start(f32[144,128]{1,0:T(8,128)} %constant.7.clone.sine) | copy-start | bytes 221188
  3.9 0.9 %copy-start.3 = (f32[144,128]{1,0:T(8,128)S(1)}, f32[144,128]{1,0:T(8,128)}, u32[]{:S(2)}) copy-start(f32[144,128]{1,0:T(8,128)} %constant.6.clone.cosine) | copy-start | bytes 221188
  4.8 0.8 %copy-start.4 = (s32[4,2048]{1,0:T(4,128)S(1)}, s32[4,2048]{1,0:T(4,128)}, u32[]{:S(2)}) copy-start(s32[4,2048]{1,0:T(4,128)} %neighbours.1) | copy-start | bytes 98308
  5.5 0.8 %copy-start.5 = (f32[8,8,128]{2,1,0:T(8,128)S(1)}, f32[8,8,128]{2,1,0:T(8,128)}, u32[]{:S(2)}) copy-start(f32[8,8,128]{2,1,0:T(8,128)} %constant.8.clone.sigmas) | copy-start | bytes 98308
  6.3 0.7 %copy-start.6 = (f32[2,2048]{1,0:T(2,128)S(1)}, f32[2,2048]{1,0:T(2,128)}, u32[]{:S(2)}) copy-start(f32[2,2048]{1,0:T(2,128)} %currents.1) | copy-start | bytes 49156
  7.0 0.7 %copy-start.7 = (f32[2,2048]{1,0:T(2,128)S(1)}, f32[2,2048]{1,0:T(2,128)}, u32[]{:S(2)}) copy-start(f32[2,2048]{1,0:T(2,128)} %winds.1) | copy-start | bytes 49156
  7.7 0.7 %copy-start.8 = (f32[2048]{0:T(1024)S(1)}, f32[2048]{0:T(1024)}, u32[]{:S(2)}) copy-start(f32[2048]{0:T(1024)} %param.11) | copy-start | bytes 24580
  8.4 0.7 %copy-start.9 = (s32[2048]{0:T(1024)S(1)}, s32[2048]{0:T(1024)}, u32[]{:S(2)}) copy-start(s32[2048]{0:T(1024)} %param.14) | copy-start | bytes 24580

commit v2 on v1

--- a/solution.py
+++ b/solution.py
@@ -163,11 +163,14 @@
 
 def wave_kernel(
     comps, tiles, rows,
-    spec, depth, currents, winds, mask, neighbours, cosine, sine, sigmas, inter,
-    out,
+    spec, inter, *refs,
+):
+    inputs, refs = refs[:8], refs[8:]
+    out, (depth, currents, winds, mask, neighbours, cosine, sine, sigmas), refs = refs[0], refs[1:9], refs[9:]
+    (
     field, cell, group, refr, slow, matrix, refracted, sq_send, sq_recv, nl_send, nl_recv, d_send, d_recv, half,
-    in_sem, mat_sem, out_sem, halo_send, halo_recv, s1, r1, s2, r2, s3, r3,
-):
+    in_sem, small_sem, mat_sem, out_sem, halo_send, halo_recv, s1, r1, s2, r2, s3, r3,
+    ) = refs
     grid_rows = 2 * comps
     bands = rows // ND
     empty = grid_rows * GW + 2 * GW
@@ -188,10 +191,20 @@
     def load(g):
         return pltpu.make_async_copy(spec.at[:, g * GW : (g + 1) * GW], field.at[g + 1], in_sem.at[g])
 
+    smalls = [
+        pltpu.make_async_copy(source, target, small_sem.at[i])
+        for i, (source, target) in enumerate(
+            zip(inputs, (depth, currents, winds, mask, neighbours, cosine, sine, sigmas))
+        )
+    ]
+    for copy in smalls:
+        copy.start()
     for g in range(grid_rows):
         load(g).start()
     matrix_copy = pltpu.make_async_copy(inter, matrix, mat_sem)
     matrix_copy.start()
+    for copy in smalls:
+        copy.wait()
 
     sigma = sigmas[me]
 
@@ -218,7 +231,6 @@
 
     for g in range(grid_rows):
         load(g).wait()
-    pl.semaphore_wait(barrier, comps + 1)
 
     def halo(buffer, which):
         return (
@@ -235,8 +247,6 @@
         )
 
     halos = halo(cell, 0) + halo(field, 2)
-    for copy in halos:
-        copy.start()
 
     row_of = lax.broadcasted_iota(jnp.int32, (rows, GW), 0)
     last_dir = functools.reduce(jnp.logical_or, [row_of == ND * b + ND - 1 for b in range(bands)])
@@ -309,6 +319,9 @@
         flow = jnp.maximum(m, 0.0) * adv + jnp.minimum(m, 0.0) * next_dir(adv)
         return adv - (flow - prev_dir(flow))
 
+    side = comps // 2
+    mine = (me // side) * side
+
     def peer(s):
         return lax.rem(me + comps // 2 + s // 2 - (s % 2) * (2 * (s // 2) + 1) + comps, comps)
 
@@ -372,7 +385,18 @@
         def send(s, carry):
             who = peer(s)
             store(who, grid_row(h, who), h, sq_send.at[h, who])
+            if h == 0:
+                @pl.when(s == 0)
+                def _():
+                    pl.semaphore_wait(barrier, comps + 1)
+
             first(h, who).start()
+            if h == 0:
+                @pl.when(s == 0)
+                def _():
+                    for copy in halos:
+                        copy.start()
+
             return carry
 
         lax.fori_loop(0, comps - 1, send, 0)
@@ -411,7 +435,7 @@
             return scale * jnp.dot(part, half[...], preferred_element_type=f32)
 
         def reply(s, carry):
-            who = peer(s)
+            who = lax.rem(me + 1 + s, comps)
             nl_send[h, who] = product(who)
             second(h, who).start()
             third(h, who).start()
@@ -438,7 +462,7 @@
         finish(h, me)
 
         def complete(s, carry):
-            who = sender(comps - 2 - s)
+            who = lax.rem(me + comps - 1 - s, comps)
             second_arrival(h, who).wait_recv()
             third_arrival(h, who).wait_recv()
             finish(h, who)
@@ -471,16 +495,19 @@
     comps, tiles = lax.axis_size("comp"), lax.axis_size("tile")
     grid_rows = cells // GW
     cosine, sine, sigmas = tables(comps, rows)
-    vmem = pl.BlockSpec(memory_space=pltpu.VMEM)
-    hbm = pl.BlockSpec(memory_space=pl.ANY)
+    hbm = pl.BlockSpec(memory_space=pltpu.HBM)
+    small = (
+        depth.reshape(1, cells), currents, winds, sea_mask.reshape(1, cells), neighbours,
+        jnp.asarray(cosine), jnp.asarray(sine), jnp.asarray(sigmas),
+    )
     f32 = jnp.float32
     dma = pltpu.SemaphoreType.DMA
     return pl.pallas_call(
         functools.partial(wave_kernel, comps, tiles, rows),
         out_shape=jax.ShapeDtypeStruct((rows, cells), f32),
-        in_specs=[hbm] + [vmem] * 8 + [hbm],
+        in_specs=[hbm] * 10,
         out_specs=hbm,
-        scratch_shapes=[
+        scratch_shapes=[pltpu.VMEM(x.shape, x.dtype) for x in small] + [
             pltpu.VMEM((grid_rows + 2, rows, GW), f32),
             pltpu.VMEM((grid_rows + 2, 8, GW), f32),
             pltpu.VMEM((grid_rows + 2, 8, GW), f32),
@@ -496,6 +523,7 @@
             pltpu.VMEM((2, comps, 1, GW), f32),
             pltpu.VMEM((comps * rows, GW), jnp.bfloat16),
             dma((grid_rows,)),
+            dma((8,)),
             dma,
             dma((2, comps)),
             dma((4,)),
@@ -508,14 +536,13 @@
             dma((2, comps)),
         ],
         compiler_params=pltpu.CompilerParams(
-            collective_id=0, has_side_effects=True, vmem_limit_bytes=32 * 1024 * 1024
+            collective_id=0, has_side_effects=True, vmem_limit_bytes=60 * 1024 * 1024
         ),
         cost_estimate=pl.CostEstimate(
             flops=2 * cells // comps * (comps * rows) ** 2, bytes_accessed=8 * rows * cells, transcendentals=0
         ),
     )(
-        spectrum, depth.reshape(1, cells), currents, winds, sea_mask.reshape(1, cells), neighbours,
-        jnp.asarray(cosine), jnp.asarray(sine), jnp.asarray(sigmas), interaction,
+        spectrum, interaction, *small,
     )
 
 

time: 68.5 us -> 59.8 us (0.87)
  local copies, waits for them, and re-layouts: 10.1 us -> 2.39 us
  Pallas kernels: 57.8 us -> 56.7 us
    unnamed x21 -> x1, local copies, waits for them, and re-layouts: 10.1 us -> 2.39 us
    pallas_call x1, Pallas kernels: 57.8 us -> 56.7 us  [fused(): pl.pallas_call(functools.partial(wave_kernel, comps, tiles, rows), out_sh...]
where the time goes in v2:
time: 59.8 us; the launch traced here: 59.1 us
  Pallas kernels  56.7 us (95%)
  local copies, waits for them, and re-layouts  2.39 us (4%)
    pallas_call x1, Pallas kernels, fused(): pl.pallas_call(functools.partial(wave_kernel, comps, tiles, rows), out_sh...  56.7 us
    unnamed x1, local copies, waits for them, and re-layouts  2.39 us

profile of v2, /device:TPU:0, one launch (start us, length us, event | category | flops | bytes accessed | tf_op | source)
XLA Modules:
  0.0 59.1 jit_solution(7003545432336647182)
XLA Ops:
  0.0 56.7 %shard_map.100 = f32[144,2048]{1,0:T(8,128)} custom-call(f32[144,2048]{1,0:T(8,128)} %spec.1, bf16[1152,1152]{1,0:T(8,128)(2,1)} %inter.1, f32[1,2048]{1,0:T(1,128)} %bitcast.2, f32[2,2048]{1,0:T(2,128)} %refs_1_.1, f32[2,2048]{1,0:T(2,128)} %refs_2_.1, s32[1,2048]{1,0:T(1,128)} %bitcast.3, s32[4,2048]{1,0:T(4,128)} %refs_4_.1, ...), custom_call_target="tpu_custom_call" | custom-call | flops 679477248 | bytes 2359296 | tf_op jit(solution)/shard_map/pallas_call | solution.py:505
  56.7 2.4 %copy.12 = f32[144,2048]{1,0:T(8,128)} copy(f32[144,2048]{1,0:T(8,128)} %shard_map.100) | data formatting | bytes 2359296
